TPU v7x, 32 devices: a whole 2x2x4 slice. The times are simulated.
32 devices in a mesh: dp: 4 (over y, x), tensor: 8 (over z, core).
Axes of the slice: x: 2, y: 2, z: 4, core: 2. Of those that a mesh axis runs over, the one named last changes fastest.
Arguments:
- tokens: bfloat16 [1024, 8192], P('dp'), may hold values from -6 to 6
- out_grad: bfloat16 [1024, 8192], P('dp'), may hold values from -6 to 6
- weight_tiles: bfloat16 [256, 2, 3, 128, 128], P(('dp', 'tensor')), may hold values from -0.125 to 0.125
- tile_places: int32 [256, 2], P(('dp', 'tensor')), may hold values from 0 to 1663, as said below
- live_counts: int32 [256], P(('dp', 'tensor')), may hold values from 0 to 2, as said below
Outputs:
- layer_out: bfloat16 [1024, 8192], P('dp', 'tensor')
- input_grad: bfloat16 [1024, 8192], P('dp', 'tensor')
Inputs may be any that keep to these rules, and one draw needn't show every extreme that they name: `tile_places`: among the slots addressed to one owner, live or not, no two have the same place; the place 64 * 26 - 1 occurs in a live slot of every owner. `live_counts`: every owner receives 2 live slots from some source, and some owner receives 2 live slots from every source; slots past the count hold padding.
All inputs are finite; a program needn't handle non-finite values.
Results may differ from a plain program's by a relative error of at most 0.012.
Values may be sent and summed in bfloat16 or wider, within the bound.
A program may use at most 192 MiB of HBM per device.

v0:
```python
import jax
import jax.numpy as jnp
from jax import lax
from jax.sharding import PartitionSpec as P

FF = 26624


def block_length(extent):
    length = min(extent, 32)
    while extent % length:
        length -= 1
    return length


def over_blocks(step, running, arrays):
    extent = arrays[0].shape[0]
    length = block_length(extent)
    shaped = tuple((item.reshape((extent // length, length) + item.shape[1:]) for item in arrays))

    def advance(acc_value, slot_block):
        return (step(acc_value, slot_block), None)

    running, _ = lax.scan(advance, running, shaped)
    return running


def body(tokens, out_grad, weight_tiles, tile_places, live_counts):
    tok_rows = tokens.shape[0]
    feat_width = tokens.shape[1]
    tile_side = weight_tiles.shape[-1]
    peer_slots = weight_tiles.shape[1]
    row_count = feat_width // tile_side
    owners = lax.axis_size("tensor")
    col_count = FF // (tile_side * owners)
    arrived_tiles, arrived_places, arrived_counts = (
        lax.all_to_all(weight_tiles, "tensor", split_axis=0, concat_axis=0, tiled=True),
        lax.all_to_all(tile_places, "tensor", split_axis=0, concat_axis=0, tiled=True),
        lax.all_to_all(live_counts, "tensor", split_axis=0, concat_axis=0, tiled=True),
    )
    slot_tiles, slot_places, slot_counts = (
        lax.all_gather(arrived_tiles, "dp", axis=0, tiled=True),
        lax.all_gather(arrived_places, "dp", axis=0, tiled=True),
        lax.all_gather(arrived_counts, "dp", axis=0, tiled=True),
    )
    slot_total = slot_places.shape[0] * peer_slots
    row_ids = (slot_places // col_count).reshape(-1).astype(jnp.int32)
    col_ids = (slot_places % col_count).reshape(-1).astype(jnp.int32)
    live_mask = (jnp.arange(peer_slots)[None, :] < slot_counts[:, None]).reshape(-1)
    flat_tiles = slot_tiles.reshape((slot_total,) + slot_tiles.shape[2:])
    flat_tiles = jnp.where(
        live_mask[:, None, None, None], flat_tiles, jnp.zeros((), flat_tiles.dtype)
    )
    slot_data = (flat_tiles, row_ids, col_ids)
    token_blocks = tokens.reshape(tok_rows, row_count, tile_side)

    def gate_up_step(acc_value, slot_block):
        weights, row_block, col_block = slot_block
        gathered = jnp.take(token_blocks, row_block, axis=1)
        products = jnp.einsum(
            "tsa,sgab->gtsb", gathered, weights[:, 0:2], preferred_element_type=jnp.float32
        )
        return acc_value.at[:, :, col_block, :].add(products)

    preact = over_blocks(
        gate_up_step, jnp.zeros((2, tok_rows, col_count, tile_side), jnp.float32), slot_data
    )
    gate_pre = preact[0]
    up_pre = preact[1]
    sigmoid_gate = jax.nn.sigmoid(gate_pre)
    gate_act = gate_pre * sigmoid_gate
    hidden = (gate_act * up_pre).astype(jnp.bfloat16)

    def down_step(acc_value, slot_block):
        weights, row_block, col_block = slot_block
        gathered = jnp.take(hidden, col_block, axis=1)
        products = jnp.einsum(
            "tsa,sab->tsb", gathered, weights[:, 2], preferred_element_type=jnp.float32
        )
        return acc_value.at[:, row_block, :].add(products)

    out_part = over_blocks(
        down_step, jnp.zeros((tok_rows, row_count, tile_side), jnp.float32), slot_data
    ).reshape(tok_rows, feat_width)
    layer_out = lax.psum_scatter(
        out_part.astype(jnp.bfloat16), "tensor", scatter_dimension=1, tiled=True
    )
    grad_blocks = out_grad.reshape(tok_rows, row_count, tile_side)

    def back_step(acc_value, slot_block):
        weights, row_block, col_block = slot_block
        gathered = jnp.take(grad_blocks, row_block, axis=1)
        products = jnp.einsum(
            "tsb,sab->tsa", gathered, weights[:, 2], preferred_element_type=jnp.float32
        )
        return acc_value.at[:, col_block, :].add(products)

    grad_hidden = over_blocks(
        back_step, jnp.zeros((tok_rows, col_count, tile_side), jnp.float32), slot_data
    )
    grad_gate = (
        grad_hidden * up_pre * (sigmoid_gate * (1.0 + gate_pre * (1.0 - sigmoid_gate)))
    ).astype(jnp.bfloat16)
    grad_up = (grad_hidden * gate_act).astype(jnp.bfloat16)
    grad_pair = jnp.stack([grad_gate, grad_up])

    def input_step(acc_value, slot_block):
        weights, row_block, col_block = slot_block
        gathered = jnp.take(grad_pair, col_block, axis=2)
        products = jnp.einsum(
            "gtsb,sgab->tsa", gathered, weights[:, 0:2], preferred_element_type=jnp.float32
        )
        return acc_value.at[:, row_block, :].add(products)

    in_part = over_blocks(
        input_step, jnp.zeros((tok_rows, row_count, tile_side), jnp.float32), slot_data
    ).reshape(tok_rows, feat_width)
    input_grad = lax.psum_scatter(
        in_part.astype(jnp.bfloat16), "tensor", scatter_dimension=1, tiled=True
    )
    return (layer_out, input_grad)


def solution(mesh):
    in_specs = (
        P("dp", None),
        P("dp", None),
        P(("dp", "tensor"), None, None, None, None),
        P(("dp", "tensor"), None),
        P(("dp", "tensor")),
    )
    out_specs = (P("dp", "tensor"), P("dp", "tensor"))
    return jax.shard_map(body, mesh=mesh, in_specs=in_specs, out_specs=out_specs, check_vma=False)
```

profile of v0, /device:TPU:0, one launch (start us, length us, event | category | flops | bytes accessed | tf_op | source)
XLA Modules:
  0.0 404.7 jit_solution(2578205139297796959)
XLA Ops:
  7.2 44.3 %all_to_all.29 = bf16[8,2,3,128,128]{4,3,2,1,0:T(8,128)(2,1)} all-to-all(bf16[8,2,3,128,128]{4,3,2,1,0:T(8,128)(2,1)} %param.17), channel_id=1, replica_groups=mesh['dp'=4,'tensor'=8] {'tensor'}, dimensions={0} | all-to-all | bytes 3145728 | tf_op jit(solution)/shard_map/all_to_all | solution.py:37
  56.3 6.7 %copy.90 = bf16[256,8192]{0,1:T(8,128)(2,1)} copy(bf16[256,8192]{1,0:T(8,128)(2,1)} %param.16) | data formatting | bytes 8388608 | tf_op args[1]
  63.0 6.4 %copy.92 = bf16[256,64,128]{2,0,1:T(8,128)(2,1)} copy(bf16[256,64,128]{0,2,1:T(8,128)(2,1)} %bitcast.209) | data formatting | bytes 8388608 | tf_op jit(solution)/shard_map/while | solution.py:24
  69.4 6.4 %copy.85 = bf16[256,8192]{0,1:T(8,128)(2,1)} copy(bf16[256,8192]{1,0:T(8,128)(2,1)} %param.15) | data formatting | bytes 8388608 | tf_op args[0]
  75.8 6.4 %copy.87 = bf16[256,64,128]{2,0,1:T(8,128)(2,1)} copy(bf16[256,64,128]{0,2,1:T(8,128)(2,1)} %bitcast.210) | data formatting | bytes 8388608 | tf_op jit(solution)/shard_map/while | solution.py:24
  83.4 5.0 %all-to-all-start = ((s32[8,1,2]{2,1,0:T(1,128)}), s32[8,1,2]{2,1,0:T(1,128)S(1)}, u32[]{:S(2)}, u32[]{:S(2)}) async-start(s32[8,1,2]{2,1,0:T(1,128)} %copy.78), calls=%async_computation | async-start | bytes 8192 | tf_op jit(solution)/shard_map/all_to_all | solution.py:38
  88.9 7.5 %all-reduce = s32[32]{0:T(128)S(1)} all-reduce(s32[32]{0:T(128)S(1)} %dynamic-update-slice), channel_id=3, replica_groups=mesh['dp'=4,'tensor'=8] {'dp'}, use_global_device_ids=true, to_apply=%add | all-reduce | flops 32 | bytes 256
  96.7 8.3 %all-gather = s32[32,1,2]{2,1,0:T(1,128)S(1)} all-gather(s32[8,1,2]{2,1,0:T(1,128)S(1)} %all-to-all-done), channel_id=2, replica_groups=mesh['dp'=4,'tensor'=8] {'dp'}, dimensions={0}, use_global_device_ids=true | all-gather | bytes 320 | tf_op jit(solution)/shard_map/all_gather | solution.py:43
  105.5 15.5 %all-gather.4.cloned.1.call-done = bf16[32,2,3,128,128]{4,3,2,1,0:T(8,128)(2,1)} async-done(((bf16[8,2,3,128,128]{4,3,2,1,0:T(8,128)(2,1)}), bf16[32,2,3,128,128]{4,3,2,1,0:T(8,128)(2,1)}) %all-gather.4.cloned.1.call-update) | async-done | bytes 6291472 | tf_op jit(solution)/shard_map/all_gather | solution.py:42
  124.3 4.5 %copy.88 = bf16[2,32,3,128,128]{4,3,1,2,0:T(8,128)(2,1)} copy(bf16[2,32,3,128,128]{4,3,2,1,0:T(8,128)(2,1)S(1)} %bitcast_select_fusion) | data formatting | bytes 12582912 | tf_op jit(solution)/shard_map/while | solution.py:24
  129.2 32.5 %while.42 = (s32[]{:T(128)}, f32[256,26,128]{2,0,1:T(8,128)S(1)}, s32[2,32]{1,0:T(2,128)S(1)}, bf16[2,32,3,128,128]{4,3,1,2,0:T(8,128)(2,1)}, s32[2,32]{1,0:T(2,...) while((s32[]{:T(128)}, f32[256,26,128]{2,0,1:T(8,128)S(1)}, s32[2,32]{1,0:T(2,128)S(1)}, ...), condition=%wide.region_9.11_spmd, body=%wide.region_7.10_spmd.sunk | while | flops 270533920 | bytes 38802964 | solution.py:24
  129.4 4.3 %gather_fusion.2 = bf16[32,256,128]{2,1,0:T(8,128)(2,1)} fusion(bf16[256,64,128]{2,0,1:T(8,128)(2,1)} %get-tuple-element.508, s32[1024]{0:T(1024)S(1)} %pad_clamp_fusion.10), kind=kCustom, calls=%fused_computation.3.clone.clone.1 | custom fusion | bytes 4194432 | tf_op jit(solution)/shard_map/while/body/eval_jaxpr/jit(_take)/gather | solution.py:92
  139.0 6.5 %scatter_fusion.2 = f32[256,26,128]{2,0,1:T(8,128)S(1)} fusion(f32[256,26,128]{2,0,1:T(8,128)S(1)} %get-tuple-element.497, s32[32]{0:T(128)S(1)} %fusion.73, f32[32,256,128]{2,1,0:T(8,128)} %fusion.74), kind=kCustom, calls=%fused_computation.7.clone.1 | custom fusion | flops 1048576 | bytes 12583040 | tf_op jit(solution)/shard_map/while/body/eval_jaxpr/scatter-add | solution.py:96
  145.5 4.3 %gather_fusion.2 = bf16[32,256,128]{2,1,0:T(8,128)(2,1)} fusion(bf16[256,64,128]{2,0,1:T(8,128)(2,1)} %get-tuple-element.508, s32[1024]{0:T(1024)S(1)} %pad_clamp_fusion.10), kind=kCustom, calls=%fused_computation.3.clone.clone.1 | custom fusion | bytes 4194432 | tf_op jit(solution)/shard_map/while/body/eval_jaxpr/jit(_take)/gather | solution.py:92
  155.1 6.5 %scatter_fusion.2 = f32[256,26,128]{2,0,1:T(8,128)S(1)} fusion(f32[256,26,128]{2,0,1:T(8,128)S(1)} %get-tuple-element.497, s32[32]{0:T(128)S(1)} %fusion.73, f32[32,256,128]{2,1,0:T(8,128)} %fusion.74), kind=kCustom, calls=%fused_computation.7.clone.1 | custom fusion | flops 1048576 | bytes 12583040 | tf_op jit(solution)/shard_map/while/body/eval_jaxpr/scatter-add | solution.py:96
  165.2 77.5 %while.40 = (s32[]{:T(128)}, f32[2,256,26,128]{3,1,2,0:T(8,128)}, s32[2,32]{1,0:T(2,128)S(1)}, bf16[2,32,3,128,128]{4,3,2,1,0:T(8,128)(2,1)}, s32[2,32]{1,0:T(2,...) while((s32[]{:T(128)}, f32[2,256,26,128]{3,1,2,0:T(8,128)}, s32[2,32]{1,0:T(2,128)S(1)}, ...), condition=%wide.region_2.4_spmd, body=%wide.region_0.3_spmd.sunk | while | flops 540017984 | bytes 59774484 | solution.py:24
  169.6 6.8 %convolution_bitcast_fusion.2 = f32[32,2,256,128]{2,3,1,0:T(8,128)} fusion(bf16[2,32,3,128,128]{4,3,2,1,0:T(8,128)(2,1)} %get-tuple-element.485, s32[]{:T(128)} %get-tuple-element.475, bf16[32,256,128]{2,1,0:T(8,128)(2,1)} %gather_fusion, pred[32]{0:T(512)(128)(4,1)S(1)} %get-tuple-element.443), kind=kOutput, calls=%fused_computation.45.clone.1 | convolution fusion | flops 537919488 | bytes 13632032 | tf_op jit(solution)/shard_map/while/body/eval_jaxpr/tsa,sgab->gtsb/dot_general | solution.py:60
  176.4 9.0 %copy.102 = f32[32,2,256,128]{3,2,1,0:T(8,128)} copy(f32[32,2,256,128]{2,3,1,0:T(8,128)} %convolution_bitcast_fusion.2) | data formatting | bytes 16777216 | tf_op jit(solution)/shard_map/while/body/eval_jaxpr/tsa,sgab->gtsb/transpose | solution.py:60
  185.4 18.7 %scatter_fusion = f32[2,256,26,128]{3,1,2,0:T(8,128)} fusion(f32[2,256,26,128]{3,1,2,0:T(8,128)} %get-tuple-element.476, s32[32]{0:T(128)S(1)} %fusion.68, f32[32,2,256,128]{3,2,1,0:T(8,128)} %copy.102), kind=kCustom, calls=%fused_computation.4.clone.1 | custom fusion | flops 2097152 | bytes 25165952 | tf_op jit(solution)/shard_map/while/body/eval_jaxpr/scatter-add | solution.py:63
  208.4 6.8 %convolution_bitcast_fusion.2 = f32[32,2,256,128]{2,3,1,0:T(8,128)} fusion(bf16[2,32,3,128,128]{4,3,2,1,0:T(8,128)(2,1)} %get-tuple-element.485, s32[]{:T(128)} %get-tuple-element.475, bf16[32,256,128]{2,1,0:T(8,128)(2,1)} %gather_fusion, pred[32]{0:T(512)(128)(4,1)S(1)} %get-tuple-element.443), kind=kOutput, calls=%fused_computation.45.clone.1 | convolution fusion | flops 537919488 | bytes 13632032 | tf_op jit(solution)/shard_map/while/body/eval_jaxpr/tsa,sgab->gtsb/dot_general | solution.py:60
  215.2 9.0 %copy.102 = f32[32,2,256,128]{3,2,1,0:T(8,128)} copy(f32[32,2,256,128]{2,3,1,0:T(8,128)} %convolution_bitcast_fusion.2) | data formatting | bytes 16777216 | tf_op jit(solution)/shard_map/while/body/eval_jaxpr/tsa,sgab->gtsb/transpose | solution.py:60
  224.2 18.6 %scatter_fusion = f32[2,256,26,128]{3,1,2,0:T(8,128)} fusion(f32[2,256,26,128]{3,1,2,0:T(8,128)} %get-tuple-element.476, s32[32]{0:T(128)S(1)} %fusion.68, f32[32,2,256,128]{3,2,1,0:T(8,128)} %copy.102), kind=kCustom, calls=%fused_computation.4.clone.1 | custom fusion | flops 2097152 | bytes 25165952 | tf_op jit(solution)/shard_map/while/body/eval_jaxpr/scatter-add | solution.py:63
  242.8 4.9 %fusion.51 = (bf16[1,256,26,128]{3,1,2,0:T(8,128)(2,1)S(1)}, bf16[1,256,26,128]{3,1,2,0:T(8,128)(2,1)S(1)}, bf16[256,26,128]{2,0,1:T(8,128)(2,1)}) fusion(f32[2,256,26,128]{3,1,2,0:T(8,128)} %get-tuple-element.131, f32[256,26,128]{2,0,1:T(8,128)S(1)} %get-tuple-element.133), kind=kLoop, calls=%fused_computation.101 | loop fusion | flops 12779520 | bytes 15335424 | tf_op jit(solution)/shard_map/stack | solution.py:105
  252.3 39.0 %while.43 = (s32[]{:T(128)}, f32[256,64,128]{2,0,1:T(8,128)}, s32[2,32]{1,0:T(2,128)S(1)}, bf16[2,32,3,128,128]{4,3,2,1,0:T(8,128)(2,1)}, s32[2,32]{1,0:T(2,128)...) while((s32[]{:T(128)}, f32[256,64,128]{2,0,1:T(8,128)}, s32[2,32]{1,0:T(2,128)S(1)}, ...), condition=%wide.region_12.14_spmd, body=%wide.region_10.13_spmd.sunk | while | flops 540018048 | bytes 54531732 | solution.py:24
  261.7 10.1 %scatter_fusion.3 = f32[256,64,128]{2,0,1:T(8,128)} fusion(f32[256,64,128]{2,0,1:T(8,128)} %get-tuple-element.539, s32[32]{0:T(128)S(1)} %get-tuple-element.466, f32[32,256,128]{2,1,0:T(8,128)} %fusion.78), kind=kCustom, calls=%fused_computation.6.clone.1 | custom fusion | flops 1048576 | bytes 12583040 | tf_op jit(solution)/shard_map/while/body/eval_jaxpr/scatter-add | solution.py:113
  281.3 10.0 %scatter_fusion.3 = f32[256,64,128]{2,0,1:T(8,128)} fusion(f32[256,64,128]{2,0,1:T(8,128)} %get-tuple-element.539, s32[32]{0:T(128)S(1)} %get-tuple-element.466, f32[32,256,128]{2,1,0:T(8,128)} %fusion.78), kind=kCustom, calls=%fused_computation.6.clone.1 | custom fusion | flops 1048576 | bytes 12583040 | tf_op jit(solution)/shard_map/while/body/eval_jaxpr/scatter-add | solution.py:113
  291.3 6.0 %copy_bitcast_fusion = bf16[256,8192]{1,0:T(8,128)(2,1)} fusion(f32[256,64,128]{2,0,1:T(8,128)} %get-tuple-element.134), kind=kLoop, calls=%fused_computation.81 | loop fusion | flops 2097152 | bytes 12582912 | tf_op jit(solution)/shard_map/convert_element_type | solution.py:119
  301.8 35.5 %while.41 = (s32[]{:T(128)}, f32[256,64,128]{2,0,1:T(8,128)}, s32[2,32]{1,0:T(2,128)S(1)}, bf16[2,32,3,128,128]{4,3,1,2,0:T(8,128)(2,1)}, s32[2,32]{1,0:T(2,128)S(1)}, /*index=5*/bf16[256,26,128]{2,0,1:T(8,128)(2,1)}, s32[]{:T(128)}) while((s32[]{:T(128)}, f32[256,64,128]{2,0,1:T(8,128)}, s32[2,32]{1,0:T(2,128)S(1)}, ...), condition=%wide.region_5.7_spmd, body=%wide.region_3.6_spmd.sunk | while | flops 270534016 | bytes 30414456 | solution.py:24
  309.4 10.2 %scatter_fusion.1 = f32[256,64,128]{2,0,1:T(8,128)} fusion(f32[256,64,128]{2,0,1:T(8,128)} %get-tuple-element.518, s32[32]{0:T(128)S(1)} %get-tuple-element.450, f32[32,256,128]{2,1,0:T(8,128)} %fusion.71), kind=kCustom, calls=%fused_computation.5.clone.1 | custom fusion | flops 1048576 | bytes 12583040 | tf_op jit(solution)/shard_map/while/body/eval_jaxpr/scatter-add | solution.py:80
  327.1 10.1 %scatter_fusion.1 = f32[256,64,128]{2,0,1:T(8,128)} fusion(f32[256,64,128]{2,0,1:T(8,128)} %get-tuple-element.518, s32[32]{0:T(128)S(1)} %get-tuple-element.450, f32[32,256,128]{2,1,0:T(8,128)} %fusion.71), kind=kCustom, calls=%fused_computation.5.clone.1 | custom fusion | flops 1048576 | bytes 12583040 | tf_op jit(solution)/shard_map/while/body/eval_jaxpr/scatter-add | solution.py:80
  337.2 6.1 %copy_bitcast_fusion.1 = bf16[256,8192]{1,0:T(8,128)(2,1)} fusion(f32[256,64,128]{2,0,1:T(8,128)} %get-tuple-element.132), kind=kLoop, calls=%fused_computation.82 | loop fusion | flops 2097152 | bytes 12582912 | tf_op jit(solution)/shard_map/convert_element_type | solution.py:86
  347.2 51.0 %reduce-scatter.3.cloned.1.call-done = bf16[256,1024]{1,0:T(8,128)(2,1)} async-done(((bf16[256,8192]{1,0:T(8,128)(2,1)}), bf16[256,1024]{1,0:T(8,128)(2,1)}) %reduce-scatter.3.cloned.1.call-update) | async-done | bytes 524304 | tf_op jit(solution)/shard_map/reduce_scatter | solution.py:85
  (92 shorter events, 80.0 us)
Async XLA Ops:
  7.2 44.4 %copy-start.4 = (s32[8]{0:T(128)S(1)}, s32[8]{0:T(128)}, u32[]{:S(2)}) copy-start(s32[8]{0:T(128)} %param.19) | copy-start | bytes 100
  7.2 48.4 %copy-start.3 = (s32[8,2]{0,1:T(2,128)S(1)}, s32[8,2]{0,1:T(2,128)}, u32[]{:S(2)}) copy-start(s32[8,2]{0,1:T(2,128)} %param.18) | copy-start | bytes 196
  7.2 113.8 %all-gather.4.cloned.1.call-start = ((), (), s32[]{:S(2)}) async-start(), calls=%async_computation.5 | async-start | bytes 7864320 | tf_op jit(solution)/shard_map/all_gather | solution.py:42
  52.2 31.2 %all-to-all-start.1 = ((s32[8,1,1]{2,1,0:T(1,128)}), s32[8,1,1]{2,1,0:T(1,128)S(1)}, u32[]{:S(2)}, u32[]{:S(2)}) async-start(s32[8,1,1]{2,1,0:T(1,128)} %copy.83), calls=%async_computation.1 | async-start | bytes 8192 | tf_op jit(solution)/shard_map/all_to_all | solution.py:39
  75.8 6.4 %copy-start.5 = (u32[32]{0:T(128)S(1)}, u32[32]{0:T(128)}, u32[]{:S(2)}) copy-start(u32[32]{0:T(128)} %constant.120) | copy-start | bytes 388
  83.4 13.3 %all-to-all-start = ((s32[8,1,2]{2,1,0:T(1,128)}), s32[8,1,2]{2,1,0:T(1,128)S(1)}, u32[]{:S(2)}, u32[]{:S(2)}) async-start(s32[8,1,2]{2,1,0:T(1,128)} %copy.78), calls=%async_computation | async-start | bytes 8192 | tf_op jit(solution)/shard_map/all_to_all | solution.py:38
  88.4 258.8 %reduce-scatter.5.cloned.1.call-start = ((), (), s32[]{:S(2)}) async-start(), calls=%async_computation.7 | async-start | bytes 4718592 | tf_op jit(solution)/shard_map/reduce_scatter | solution.py:118
  124.3 4.5 %copy-start = (bf16[2,32,3,128,128]{4,3,2,1,0:T(8,128)(2,1)}, bf16[2,32,3,128,128]{4,3,2,1,0:T(8,128)(2,1)S(1)}, u32[]{:S(2)}) copy-start(bf16[2,32,3,128,128]{4,3,2,1,0:T(8,128)(2,1)S(1)} %bitcast_select_fusion) | copy-start | bytes 18874372
  133.7 2.5 copy-start.1
  149.9 2.5 copy-start.1
  255.3 3.1 copy-start.2
  274.9 3.1 copy-start.2
  297.2 101.0 %reduce-scatter.3.cloned.1.call-start = ((), (), s32[]{:S(2)}) async-start(), calls=%async_computation.6 | async-start | bytes 4718592 | tf_op jit(solution)/shard_map/reduce_scatter | solution.py:85
Sparse Core Ops, SparseCore 0:
  51.6 69.3 all-gather.3
  297.4 49.7 reduce-scatter.4
  350.0 48.1 reduce-scatter.2
where the time goes:
time: 407 us; the launch traced here: 405 us
  other arithmetic  112 us (28%)
  local copies, waits for them, and re-layouts  108 us (27%)
  waiting for transfers between devices  70.5 us (17%)
  blocking collectives  60.1 us (15%)
  matrix products  30.9 us (8%)
  between operations  14.5 us (4%)
  starting transfers between devices  8.66 us (2%)
    reduce_scatter x1, waiting for transfers between devices, body(): lax.psum_scatter(out_part.astype(jnp.bfloat16), 'tensor', scatter_dimensi...  51 us
    all_to_all x1, blocking collectives, body(): lax.all_to_all(weight_tiles, 'tensor', split_axis=0, concat_axis=0, tiled...  44.3 us
    scatter-add x2, other arithmetic, gate_up_step(): return acc_value.at[:, :, col_block, :].add(products)  37.3 us
    scatter-add x2, other arithmetic, down_step(): return acc_value.at[:, row_block, :].add(products)  20.3 us
    scatter-add x2, other arithmetic, input_step(): return acc_value.at[:, row_block, :].add(products)  20.1 us
    transpose x2, local copies, waits for them, and re-layouts, gate_up_step(): jnp.einsum('tsa,sgab->gtsb', gathered, weights[:, 0:2], preferred_element...  17.9 us
    while x3, local copies, waits for them, and re-layouts, over_blocks(): running, _ = lax.scan(advance, running, shaped)  17.3 us
    all_gather x1, waiting for transfers between devices, body(): lax.all_gather(arrived_tiles, 'dp', axis=0, tiled=True)  15.5 us
  transfers between devices with their start and end apart: 5, of which 3 were waited for; matrix products, arithmetic and copies ran while one was open for 18% of the time, Pallas kernels for 0%

commit v1 on v0

--- a/solution.py
+++ b/solution.py
@@ -33,8 +33,24 @@
     row_count = feat_width // tile_side
     owners = lax.axis_size("tensor")
     col_count = FF // (tile_side * owners)
+
+    def check_words_for(inputs, link_axis, dim_i, which_dim):
+        k_now, outer = (jax.lax.axis_size(link_axis), jax.lax.axis_index(link_axis))
+        field_out = inputs.shape[dim_i] // k_now
+        piece_now = jnp.roll(inputs, -outer * field_out, dim_i)
+        shelf = [lax.slice_in_dim(piece_now, 0, field_out, axis=dim_i)]
+        for u in range(1, k_now):
+            taken_in = lax.slice_in_dim(piece_now, u * field_out, (u + 1) * field_out, axis=dim_i)
+            shelf.append(
+                jax.lax.ppermute(
+                    taken_in, link_axis, perm=[(pp, (pp + u) % k_now) for pp in range(k_now)]
+                )
+            )
+        passed = jnp.concatenate(shelf[::-1], which_dim)
+        return jnp.roll(passed, (outer + 1) * shelf[0].shape[which_dim], which_dim)
+
     arrived_tiles, arrived_places, arrived_counts = (
-        lax.all_to_all(weight_tiles, "tensor", split_axis=0, concat_axis=0, tiled=True),
+        check_words_for(weight_tiles, "tensor", 0, 0),
         lax.all_to_all(tile_places, "tensor", split_axis=0, concat_axis=0, tiled=True),
         lax.all_to_all(live_counts, "tensor", split_axis=0, concat_axis=0, tiled=True),
     )

time: 407 us -> 405 us (level)
  blocking collectives: 60.1 us -> 15.8 us
  waiting for transfers between devices: 70.5 us -> 102 us
  starting transfers between devices: 8.66 us -> 18 us
    all_to_all x1 -> x0, blocking collectives: 44.3 us -> none  [body(): lax.all_to_all(weight_tiles, 'tensor', split_axis=0, concat_axis=0, tiled...]
    ppermute x0 -> x7, waiting for transfers between devices: none -> 31.5 us  [check_words_for(): jax.lax.ppermute(taken_in, link_axis, perm=[(pp, (pp + u) % k_now) for pp...]
    ppermute x0 -> x7, starting transfers between devices: none -> 7.8 us  [check_words_for(): jax.lax.ppermute(taken_in, link_axis, perm=[(pp, (pp + u) % k_now) for pp...]
    unnamed x13 -> x20, local copies, waits for them, and re-layouts: 13.9 us -> 14.2 us
  transfers between devices with their start and end apart: 5 -> 12, of which waited for: 3 -> 7; matrix products, arithmetic and copies ran while one was open for 18% -> 19% of each run, Pallas kernels for 0% -> 0%
where the time goes in v1:
time: 405 us; the launch traced here: 403 us
  other arithmetic  115 us (28%)
  local copies, waits for them, and re-layouts  107 us (26%)
  waiting for transfers between devices  102 us (25%)
  matrix products  29.7 us (7%)
  starting transfers between devices  18 us (4%)
  blocking collectives  15.8 us (4%)
  between operations  14.7 us (4%)
    reduce_scatter x1, waiting for transfers between devices, body(): lax.psum_scatter(out_part.astype(jnp.bfloat16), 'tensor', scatter_dimensi...  51 us
    scatter-add x2, other arithmetic, gate_up_step(): return acc_value.at[:, :, col_block, :].add(products)  37.3 us
    ppermute x7, waiting for transfers between devices, check_words_for(): jax.lax.ppermute(taken_in, link_axis, perm=[(pp, (pp + u) % k_now) for pp...  31.5 us
    scatter-add x2, other arithmetic, down_step(): return acc_value.at[:, row_block, :].add(products)  20.3 us
    scatter-add x2, other arithmetic, input_step(): return acc_value.at[:, row_block, :].add(products)  20.1 us
    transpose x2, local copies, waits for them, and re-layouts, gate_up_step(): jnp.einsum('tsa,sgab->gtsb', gathered, weights[:, 0:2], preferred_element...  18 us
    while x3, local copies, waits for them, and re-layouts, over_blocks(): running, _ = lax.scan(advance, running, shaped)  17.3 us
    all_gather x1, waiting for transfers between devices, body(): lax.all_gather(arrived_tiles, 'dp', axis=0, tiled=True)  16 us
  transfers between devices with their start and end apart: 12, of which 7 were waited for; matrix products, arithmetic and copies ran while one was open for 19% of the time, Pallas kernels for 0%

profile of v1, /device:TPU:0, one launch (start us, length us, event | category | flops | bytes accessed | tf_op | source)
XLA Modules:
  0.0 403.3 jit_solution(4191350464366508292)
XLA Ops:
  10.1 4.5 %collective-permute-start = (bf16[1,2,3,128,128]{4,3,2,1,0:T(8,128)(2,1)}, bf16[1,2,3,128,128]{4,3,2,1,0:T(8,128)(2,1)S(1)}, u32[]{:S(2)}, u32[]{:S(2)}) collective-permute-start(bf16[1,2,3,128,128]{4,3,2,1,0:T(8,128)(2,1)} %get-tuple-element.309), channel_id=1, source_target_pairs={{0,7},{1,0},{2,1},{3,2},{4,3},{5,4},{6,5},{7,6},{8,15},{9,8},{10,9... | collective-permute-start | bytes 589832 | tf_op jit(solution)/shard_map/ppermute | solution.py:45
  28.7 20.9 %collective-permute-done.3 = bf16[1,2,3,128,128]{4,3,2,1,0:T(8,128)(2,1)S(1)} collective-permute-done((bf16[1,2,3,128,128]{4,3,2,1,0:T(8,128)(2,1)S(1)}, bf16[1,2,3,128,128]{4,3,2,1,0:T(8,128)(2,1)S(1)}, u32[]{:S(2)}, u32[]{:S(2)}) %collective-permute-start.3) | collective-permute-done | bytes 196640 | tf_op jit(solution)/shard_map/ppermute | solution.py:45
  52.2 4.7 %all-to-all-start.1 = ((s32[8,1,1]{2,1,0:T(1,128)}), s32[8,1,1]{2,1,0:T(1,128)S(1)}, u32[]{:S(2)}, u32[]{:S(2)}) async-start(s32[8,1,1]{2,1,0:T(1,128)} %copy.83), calls=%async_computation.1 | async-start | bytes 8192 | tf_op jit(solution)/shard_map/all_to_all | solution.py:55
  57.7 6.6 %copy.85 = bf16[256,8192]{0,1:T(8,128)(2,1)} copy(bf16[256,8192]{1,0:T(8,128)(2,1)} %param.17) | data formatting | bytes 8388608 | tf_op args[0]
  64.3 6.4 %copy.87 = bf16[256,64,128]{2,0,1:T(8,128)(2,1)} copy(bf16[256,64,128]{0,2,1:T(8,128)(2,1)} %bitcast.209) | data formatting | bytes 8388608 | tf_op jit(solution)/shard_map/while | solution.py:24
  70.7 6.4 %copy.90 = bf16[256,8192]{0,1:T(8,128)(2,1)} copy(bf16[256,8192]{1,0:T(8,128)(2,1)} %param.18) | data formatting | bytes 8388608 | tf_op args[1]
  77.1 6.4 %copy.92 = bf16[256,64,128]{2,0,1:T(8,128)(2,1)} copy(bf16[256,64,128]{0,2,1:T(8,128)(2,1)} %bitcast.210) | data formatting | bytes 8388608 | tf_op jit(solution)/shard_map/while | solution.py:24
  84.9 5.2 %all-to-all-start = ((s32[8,1,2]{2,1,0:T(1,128)}), s32[8,1,2]{2,1,0:T(1,128)S(1)}, u32[]{:S(2)}, u32[]{:S(2)}) async-start(s32[8,1,2]{2,1,0:T(1,128)} %copy.78), calls=%async_computation | async-start | bytes 8192 | tf_op jit(solution)/shard_map/all_to_all | solution.py:54
  90.6 7.5 %all-reduce = s32[32]{0:T(128)S(1)} all-reduce(s32[32]{0:T(128)S(1)} %dynamic-update-slice), channel_id=3, replica_groups=mesh['dp'=4,'tensor'=8] {'dp'}, use_global_device_ids=true, to_apply=%add | all-reduce | flops 32 | bytes 256
  98.4 8.3 %all-gather = s32[32,1,2]{2,1,0:T(1,128)S(1)} all-gather(s32[8,1,2]{2,1,0:T(1,128)S(1)} %all-to-all-done), channel_id=2, replica_groups=mesh['dp'=4,'tensor'=8] {'dp'}, dimensions={0}, use_global_device_ids=true | all-gather | bytes 320 | tf_op jit(solution)/shard_map/all_gather | solution.py:59
  107.2 16.0 %all-gather.4.cloned.1.call-done = bf16[32,2,3,128,128]{4,3,2,1,0:T(8,128)(2,1)} async-done(((bf16[8,2,3,128,128]{4,3,2,1,0:T(8,128)(2,1)}), bf16[32,2,3,128,128]{4,3,2,1,0:T(8,128)(2,1)}) %all-gather.4.cloned.1.call-update) | async-done | bytes 6291472 | tf_op jit(solution)/shard_map/all_gather | solution.py:58
  126.4 4.5 %copy.88 = bf16[2,32,3,128,128]{4,3,1,2,0:T(8,128)(2,1)} copy(bf16[2,32,3,128,128]{4,3,2,1,0:T(8,128)(2,1)S(1)} %bitcast_select_fusion) | data formatting | bytes 12582912 | tf_op jit(solution)/shard_map/while | solution.py:24
  134.6 74.1 %while.40 = (s32[]{:T(128)}, f32[2,256,26,128]{3,1,2,0:T(8,128)}, s32[2,32]{1,0:T(2,128)S(1)}, bf16[2,32,3,128,128]{4,3,2,1,0:T(8,128)(2,1)}, s32[2,32]{1,0:T(2,...) while((s32[]{:T(128)}, f32[2,256,26,128]{3,1,2,0:T(8,128)}, s32[2,32]{1,0:T(2,128)S(1)}, ...), condition=%wide.region_2.5_spmd, body=%wide.region_0.4_spmd.sunk | while | flops 540017984 | bytes 59774484 | solution.py:24
  137.8 6.2 %convolution_bitcast_fusion.2 = f32[32,2,256,128]{2,3,1,0:T(8,128)} fusion(bf16[2,32,3,128,128]{4,3,2,1,0:T(8,128)(2,1)} %get-tuple-element.493, s32[]{:T(128)} %get-tuple-element.483, bf16[32,256,128]{2,1,0:T(8,128)(2,1)S(1)} %gather_fusion, pred[32]{0:T(512)(128)(4,1)S(1)} %get-tuple-element.451), kind=kOutput, calls=%fused_computation.45.clone.1 | convolution fusion | flops 537919488 | bytes 13632032 | tf_op jit(solution)/shard_map/while/body/eval_jaxpr/tsa,sgab->gtsb/dot_general | solution.py:76
  144.0 9.0 %copy.102 = f32[32,2,256,128]{3,2,1,0:T(8,128)} copy(f32[32,2,256,128]{2,3,1,0:T(8,128)} %convolution_bitcast_fusion.2) | data formatting | bytes 16777216 | tf_op jit(solution)/shard_map/while/body/eval_jaxpr/tsa,sgab->gtsb/transpose | solution.py:76
  153.0 18.7 %scatter_fusion = f32[2,256,26,128]{3,1,2,0:T(8,128)} fusion(f32[2,256,26,128]{3,1,2,0:T(8,128)} %get-tuple-element.484, s32[32]{0:T(128)S(1)} %fusion.71, f32[32,2,256,128]{3,2,1,0:T(8,128)} %copy.102), kind=kCustom, calls=%fused_computation.4.clone.1 | custom fusion | flops 2097152 | bytes 25165952 | tf_op jit(solution)/shard_map/while/body/eval_jaxpr/scatter-add | solution.py:79
  174.9 6.2 %convolution_bitcast_fusion.2 = f32[32,2,256,128]{2,3,1,0:T(8,128)} fusion(bf16[2,32,3,128,128]{4,3,2,1,0:T(8,128)(2,1)} %get-tuple-element.493, s32[]{:T(128)} %get-tuple-element.483, bf16[32,256,128]{2,1,0:T(8,128)(2,1)S(1)} %gather_fusion, pred[32]{0:T(512)(128)(4,1)S(1)} %get-tuple-element.451), kind=kOutput, calls=%fused_computation.45.clone.1 | convolution fusion | flops 537919488 | bytes 13632032 | tf_op jit(solution)/shard_map/while/body/eval_jaxpr/tsa,sgab->gtsb/dot_general | solution.py:76
  181.1 9.0 %copy.102 = f32[32,2,256,128]{3,2,1,0:T(8,128)} copy(f32[32,2,256,128]{2,3,1,0:T(8,128)} %convolution_bitcast_fusion.2) | data formatting | bytes 16777216 | tf_op jit(solution)/shard_map/while/body/eval_jaxpr/tsa,sgab->gtsb/transpose | solution.py:76
  190.1 18.6 %scatter_fusion = f32[2,256,26,128]{3,1,2,0:T(8,128)} fusion(f32[2,256,26,128]{3,1,2,0:T(8,128)} %get-tuple-element.484, s32[32]{0:T(128)S(1)} %fusion.71, f32[32,2,256,128]{3,2,1,0:T(8,128)} %copy.102), kind=kCustom, calls=%fused_computation.4.clone.1 | custom fusion | flops 2097152 | bytes 25165952 | tf_op jit(solution)/shard_map/while/body/eval_jaxpr/scatter-add | solution.py:79
  209.0 32.3 %while.42 = (s32[]{:T(128)}, f32[256,26,128]{2,0,1:T(8,128)S(1)}, s32[2,32]{1,0:T(2,128)S(1)}, bf16[2,32,3,128,128]{4,3,1,2,0:T(8,128)(2,1)}, s32[2,32]{1,0:T(2,...) while((s32[]{:T(128)}, f32[256,26,128]{2,0,1:T(8,128)S(1)}, s32[2,32]{1,0:T(2,128)S(1)}, ...), condition=%wide.region_9.12_spmd, body=%wide.region_7.11_spmd.sunk | while | flops 270533920 | bytes 38802964 | solution.py:24
  218.7 6.5 %scatter_fusion.2 = f32[256,26,128]{2,0,1:T(8,128)S(1)} fusion(f32[256,26,128]{2,0,1:T(8,128)S(1)} %get-tuple-element.505, s32[32]{0:T(128)S(1)} %fusion.76, f32[32,256,128]{2,1,0:T(8,128)} %fusion.77), kind=kCustom, calls=%fused_computation.7.clone.1 | custom fusion | flops 1048576 | bytes 12583040 | tf_op jit(solution)/shard_map/while/body/eval_jaxpr/scatter-add | solution.py:112
  234.8 6.5 %scatter_fusion.2 = f32[256,26,128]{2,0,1:T(8,128)S(1)} fusion(f32[256,26,128]{2,0,1:T(8,128)S(1)} %get-tuple-element.505, s32[32]{0:T(128)S(1)} %fusion.76, f32[32,256,128]{2,1,0:T(8,128)} %fusion.77), kind=kCustom, calls=%fused_computation.7.clone.1 | custom fusion | flops 1048576 | bytes 12583040 | tf_op jit(solution)/shard_map/while/body/eval_jaxpr/scatter-add | solution.py:112
  241.3 4.9 %fusion.51 = (bf16[1,256,26,128]{3,1,2,0:T(8,128)(2,1)S(1)}, bf16[1,256,26,128]{3,1,2,0:T(8,128)(2,1)S(1)}, bf16[256,26,128]{2,0,1:T(8,128)(2,1)}) fusion(f32[2,256,26,128]{3,1,2,0:T(8,128)} %get-tuple-element.132, f32[256,26,128]{2,0,1:T(8,128)S(1)} %get-tuple-element.134), kind=kLoop, calls=%fused_computation.105 | loop fusion | flops 12779520 | bytes 15335424 | tf_op jit(solution)/shard_map/stack | solution.py:121
  250.8 39.0 %while.43 = (s32[]{:T(128)}, f32[256,64,128]{2,0,1:T(8,128)}, s32[2,32]{1,0:T(2,128)S(1)}, bf16[2,32,3,128,128]{4,3,2,1,0:T(8,128)(2,1)}, s32[2,32]{1,0:T(2,128)...) while((s32[]{:T(128)}, f32[256,64,128]{2,0,1:T(8,128)}, s32[2,32]{1,0:T(2,128)S(1)}, ...), condition=%wide.region_12.15_spmd, body=%wide.region_10.14_spmd.sunk | while | flops 540018048 | bytes 54531732 | solution.py:24
  260.3 10.1 %scatter_fusion.3 = f32[256,64,128]{2,0,1:T(8,128)} fusion(f32[256,64,128]{2,0,1:T(8,128)} %get-tuple-element.547, s32[32]{0:T(128)S(1)} %get-tuple-element.474, f32[32,256,128]{2,1,0:T(8,128)} %fusion.81), kind=kCustom, calls=%fused_computation.6.clone.1 | custom fusion | flops 1048576 | bytes 12583040 | tf_op jit(solution)/shard_map/while/body/eval_jaxpr/scatter-add | solution.py:129
  279.8 10.0 %scatter_fusion.3 = f32[256,64,128]{2,0,1:T(8,128)} fusion(f32[256,64,128]{2,0,1:T(8,128)} %get-tuple-element.547, s32[32]{0:T(128)S(1)} %get-tuple-element.474, f32[32,256,128]{2,1,0:T(8,128)} %fusion.81), kind=kCustom, calls=%fused_computation.6.clone.1 | custom fusion | flops 1048576 | bytes 12583040 | tf_op jit(solution)/shard_map/while/body/eval_jaxpr/scatter-add | solution.py:129
  289.9 6.0 %copy_bitcast_fusion = bf16[256,8192]{1,0:T(8,128)(2,1)} fusion(f32[256,64,128]{2,0,1:T(8,128)} %get-tuple-element.135), kind=kLoop, calls=%fused_computation.81 | loop fusion | flops 2097152 | bytes 12582912 | tf_op jit(solution)/shard_map/convert_element_type | solution.py:135
  300.4 35.5 %while.41 = (s32[]{:T(128)}, f32[256,64,128]{2,0,1:T(8,128)}, s32[2,32]{1,0:T(2,128)S(1)}, bf16[2,32,3,128,128]{4,3,1,2,0:T(8,128)(2,1)}, s32[2,32]{1,0:T(2,128)S(1)}, /*index=5*/bf16[256,26,128]{2,0,1:T(8,128)(2,1)}, s32[]{:T(128)}) while((s32[]{:T(128)}, f32[256,64,128]{2,0,1:T(8,128)}, s32[2,32]{1,0:T(2,128)S(1)}, ...), condition=%wide.region_5.8_spmd, body=%wide.region_3.7_spmd.sunk | while | flops 270534016 | bytes 30414456 | solution.py:24
  308.1 10.2 %scatter_fusion.1 = f32[256,64,128]{2,0,1:T(8,128)} fusion(f32[256,64,128]{2,0,1:T(8,128)} %get-tuple-element.526, s32[32]{0:T(128)S(1)} %get-tuple-element.458, f32[32,256,128]{2,1,0:T(8,128)} %fusion.74), kind=kCustom, calls=%fused_computation.5.clone.1 | custom fusion | flops 1048576 | bytes 12583040 | tf_op jit(solution)/shard_map/while/body/eval_jaxpr/scatter-add | solution.py:96
  325.8 10.1 %scatter_fusion.1 = f32[256,64,128]{2,0,1:T(8,128)} fusion(f32[256,64,128]{2,0,1:T(8,128)} %get-tuple-element.526, s32[32]{0:T(128)S(1)} %get-tuple-element.458, f32[32,256,128]{2,1,0:T(8,128)} %fusion.74), kind=kCustom, calls=%fused_computation.5.clone.1 | custom fusion | flops 1048576 | bytes 12583040 | tf_op jit(solution)/shard_map/while/body/eval_jaxpr/scatter-add | solution.py:96
  335.9 6.0 %copy_bitcast_fusion.1 = bf16[256,8192]{1,0:T(8,128)(2,1)} fusion(f32[256,64,128]{2,0,1:T(8,128)} %get-tuple-element.133), kind=kLoop, calls=%fused_computation.82 | loop fusion | flops 2097152 | bytes 12582912 | tf_op jit(solution)/shard_map/convert_element_type | solution.py:102
  345.7 51.0 %reduce-scatter.3.cloned.1.call-done = bf16[256,1024]{1,0:T(8,128)(2,1)} async-done(((bf16[256,8192]{1,0:T(8,128)(2,1)}), bf16[256,1024]{1,0:T(8,128)(2,1)}) %reduce-scatter.3.cloned.1.call-update) | async-done | bytes 524304 | tf_op jit(solution)/shard_map/reduce_scatter | solution.py:101
  (116 shorter events, 101.8 us)
Async XLA Ops:
  7.2 116.0 %all-gather.4.cloned.1.call-start = ((), (), s32[]{:S(2)}) async-start(), calls=%async_computation.4 | async-start | bytes 7864320 | tf_op jit(solution)/shard_map/all_gather | solution.py:58
  10.1 10.1 %collective-permute-start = (bf16[1,2,3,128,128]{4,3,2,1,0:T(8,128)(2,1)}, bf16[1,2,3,128,128]{4,3,2,1,0:T(8,128)(2,1)S(1)}, u32[]{:S(2)}, u32[]{:S(2)}) collective-permute-start(bf16[1,2,3,128,128]{4,3,2,1,0:T(8,128)(2,1)} %get-tuple-element.309), channel_id=1, source_target_pairs={{0,7},{1,0},{2,1},{3,2},{4,3},{5,4},{6,5},{7,6},{8,15},{9,8},{10,9... | collective-permute-start | bytes 589832 | tf_op jit(solution)/shard_map/ppermute | solution.py:45
  14.6 9.9 %collective-permute-start.1 = (bf16[1,2,3,128,128]{4,3,2,1,0:T(8,128)(2,1)}, bf16[1,2,3,128,128]{4,3,2,1,0:T(8,128)(2,1)S(1)}, u32[]{:S(2)}, u32[]{:S(2)}) collective-permute-start(bf16[1,2,3,128,128]{4,3,2,1,0:T(8,128)(2,1)} %get-tuple-element.308), channel_id=1, source_target_pairs={{0,6},{1,7},{2,0},{3,1},{4,2},{5,3},{6,4},{7,5},{8,14},{9,15},{10,... | collective-permute-start | bytes 589832 | tf_op jit(solution)/shard_map/ppermute | solution.py:45
  15.1 13.5 %collective-permute-start.2 = (bf16[1,2,3,128,128]{4,3,2,1,0:T(8,128)(2,1)S(1)}, bf16[1,2,3,128,128]{4,3,2,1,0:T(8,128)(2,1)S(1)}, u32[]{:S(2)}, u32[]{:S(2)}) collective-permute-start(bf16[1,2,3,128,128]{4,3,2,1,0:T(8,128)(2,1)S(1)} %get-tuple-element.307), channel_id=1, source_target_pairs={{0,5},{1,6},{2,7},{3,0},{4,1},{5,2},{6,3},{7,4},{8,13},{9,14},{10,... | collective-permute-start | bytes 589832 | tf_op jit(solution)/shard_map/ppermute | solution.py:45
  15.1 34.4 %collective-permute-start.3 = (bf16[1,2,3,128,128]{4,3,2,1,0:T(8,128)(2,1)S(1)}, bf16[1,2,3,128,128]{4,3,2,1,0:T(8,128)(2,1)S(1)}, u32[]{:S(2)}, u32[]{:S(2)}) collective-permute-start(bf16[1,2,3,128,128]{4,3,2,1,0:T(8,128)(2,1)S(1)} %get-tuple-element.306), channel_id=1, source_target_pairs={{0,4},{1,5},{2,6},{3,7},{4,0},{5,1},{6,2},{7,3},{8,12},{9,13},{10,... | collective-permute-start | bytes 589832 | tf_op jit(solution)/shard_map/ppermute | solution.py:45
  17.9 31.7 %collective-permute-start.4 = (bf16[1,2,3,128,128]{4,3,2,1,0:T(8,128)(2,1)S(1)}, bf16[1,2,3,128,128]{4,3,2,1,0:T(8,128)(2,1)S(1)}, u32[]{:S(2)}, u32[]{:S(2)}) collective-permute-start(bf16[1,2,3,128,128]{4,3,2,1,0:T(8,128)(2,1)S(1)} %get-tuple-element.305), channel_id=1, source_target_pairs={{0,3},{1,4},{2,5},{3,6},{4,7},{5,0},{6,1},{7,2},{8,11},{9,12},{10,... | collective-permute-start | bytes 589832 | tf_op jit(solution)/shard_map/ppermute | solution.py:45
  20.2 29.4 %collective-permute-start.5 = (bf16[1,2,3,128,128]{4,3,2,1,0:T(8,128)(2,1)S(1)}, bf16[1,2,3,128,128]{4,3,2,1,0:T(8,128)(2,1)S(1)}, u32[]{:S(2)}, u32[]{:S(2)}) collective-permute-start(bf16[1,2,3,128,128]{4,3,2,1,0:T(8,128)(2,1)S(1)} %get-tuple-element.304), channel_id=1, source_target_pairs={{0,2},{1,3},{2,4},{3,5},{4,6},{5,7},{6,0},{7,1},{8,10},{9,11},{10,... | collective-permute-start | bytes 589832 | tf_op jit(solution)/shard_map/ppermute | solution.py:45
  24.5 25.2 %collective-permute-start.6 = (bf16[1,2,3,128,128]{4,3,2,1,0:T(8,128)(2,1)S(1)}, bf16[1,2,3,128,128]{4,3,2,1,0:T(8,128)(2,1)S(1)}, u32[]{:S(2)}, u32[]{:S(2)}) collective-permute-start(bf16[1,2,3,128,128]{4,3,2,1,0:T(8,128)(2,1)S(1)} %get-tuple-element.303), channel_id=1, source_target_pairs={{0,1},{1,2},{2,3},{3,4},{4,5},{5,6},{6,7},{7,0},{8,9},{9,10},{10,1... | collective-permute-start | bytes 589832 | tf_op jit(solution)/shard_map/ppermute | solution.py:45
  28.6 22.9 %copy-start.4 = (s32[8]{0:T(128)S(1)}, s32[8]{0:T(128)}, u32[]{:S(2)}) copy-start(s32[8]{0:T(128)} %param.21) | copy-start | bytes 100
  28.6 28.3 %copy-start.3 = (s32[8,2]{0,1:T(2,128)S(1)}, s32[8,2]{0,1:T(2,128)}, u32[]{:S(2)}) copy-start(s32[8,2]{0,1:T(2,128)} %param.20) | copy-start | bytes 196
  52.2 32.7 %all-to-all-start.1 = ((s32[8,1,1]{2,1,0:T(1,128)}), s32[8,1,1]{2,1,0:T(1,128)S(1)}, u32[]{:S(2)}, u32[]{:S(2)}) async-start(s32[8,1,1]{2,1,0:T(1,128)} %copy.83), calls=%async_computation.1 | async-start | bytes 8192 | tf_op jit(solution)/shard_map/all_to_all | solution.py:55
  77.1 6.4 %copy-start.5 = (u32[32]{0:T(128)S(1)}, u32[32]{0:T(128)}, u32[]{:S(2)}) copy-start(u32[32]{0:T(128)} %constant.142) | copy-start | bytes 388
  84.9 13.4 %all-to-all-start = ((s32[8,1,2]{2,1,0:T(1,128)}), s32[8,1,2]{2,1,0:T(1,128)S(1)}, u32[]{:S(2)}, u32[]{:S(2)}) async-start(s32[8,1,2]{2,1,0:T(1,128)} %copy.78), calls=%async_computation | async-start | bytes 8192 | tf_op jit(solution)/shard_map/all_to_all | solution.py:54
  90.1 255.7 %reduce-scatter.5.cloned.1.call-start = ((), (), s32[]{:S(2)}) async-start(), calls=%async_computation.6 | async-start | bytes 4718592 | tf_op jit(solution)/shard_map/reduce_scatter | solution.py:134
  126.4 4.5 %copy-start = (bf16[2,32,3,128,128]{4,3,2,1,0:T(8,128)(2,1)}, bf16[2,32,3,128,128]{4,3,2,1,0:T(8,128)(2,1)S(1)}, u32[]{:S(2)}) copy-start(bf16[2,32,3,128,128]{4,3,2,1,0:T(8,128)(2,1)S(1)} %bitcast_select_fusion) | copy-start | bytes 18874372
  213.4 2.5 copy-start.1
  229.6 2.5 copy-start.1
  253.9 3.1 copy-start.2
  273.4 3.1 copy-start.2
  295.9 100.9 %reduce-scatter.3.cloned.1.call-start = ((), (), s32[]{:S(2)}) async-start(), calls=%async_computation.5 | async-start | bytes 4718592 | tf_op jit(solution)/shard_map/reduce_scatter | solution.py:101
Sparse Core Ops, SparseCore 0:
  51.6 71.4 all-gather.3
  296.0 49.6 reduce-scatter.4
  348.6 48.1 reduce-scatter.2
